TPU v7x, 256 devices: a whole 4x4x8 slice. The times are simulated.
256 devices in a mesh: wide: 64 (over x, z, core), narrow: 4 (over y).
Axes of the slice: x: 4, y: 4, z: 8, core: 2. Of those that a mesh axis runs over, the one named last changes fastest.
Arguments:
- dosage: bfloat16 [262144, 4096], P(('wide', 'narrow')), may hold values from 0 to 2
- keep_rows: int32 [229376], P(('wide', 'narrow')), may hold values from 0 to 1023, as said below
- allele_counts: int32 [4096], replicated, may hold values from 157286 to 367000, as said below
- projection: bfloat16 [4096, 128], replicated, may hold values from -0.09375 to 0.09375
Outputs:
- scores: float32 [229376, 128], P(('wide', 'narrow'))
- loadings: float32 [4096, 128], P('narrow')
Inputs may be any that keep to these rules, and one draw needn't show every extreme that they name: `keep_rows`: each block of 896 entries holds distinct local row numbers of one device's 1024 samples, ascending. `allele_counts`: totals over all 262144 genotyped samples, before outlier removal.
All inputs are finite; a program needn't handle non-finite values.
Results may differ from a plain program's by a relative error of at most 0.0075.
The roundings to bfloat16 on the way count: a program that leaves them out, or rounds other values in their place, can miss the bound.
Values sent between devices are 32-bit elements; how exact they have to be, the bound alone decides.
A program may use at most 64 MiB of HBM per device.

v0:
```python
import math

import jax
import jax.numpy as jnp
from jax import lax
from jax.sharding import PartitionSpec as P

ITERS = 2


def transposed_product(left_side, right_side):
    return lax.dot_general(
        left_side, right_side, (((0,), (0,)), ((), ())), preferred_element_type=jnp.float32
    )


def invert_factor(gram_matrix):
    lower_factor = jnp.linalg.cholesky(gram_matrix)
    unit_matrix = jnp.eye(gram_matrix.shape[0], dtype=jnp.float32)
    return jax.scipy.linalg.solve_triangular(lower_factor, unit_matrix, lower=True)


def on_device(dosage, keep_rows, allele_counts, projection):
    groups = lax.axis_size("wide") * lax.axis_size("narrow")
    samples_total = dosage.shape[0] * groups
    kept_total = keep_rows.shape[0] * groups
    snp_count = dosage.shape[1]
    narrow_size = lax.axis_size("narrow")
    share_rows = snp_count // narrow_size
    position = lax.axis_index("narrow")
    frequency = allele_counts.astype(jnp.float32) / (2.0 * samples_total)
    center = 2.0 * frequency
    spread = jnp.sqrt(2.0 * frequency * (1.0 - frequency))
    chosen = jnp.take(dosage, keep_rows, axis=0)
    standard = ((chosen.astype(jnp.float32) - center) / spread).astype(jnp.bfloat16)
    projected = jnp.dot(standard, projection, preferred_element_type=jnp.float32).astype(
        jnp.bfloat16
    )
    inverse = None
    loadings = None
    for iteration in range(ITERS):
        last_turn = iteration + 1 == ITERS
        gram_matrix = None
        gram_matrix = lax.psum(transposed_product(projected, projected), ("wide", "narrow"))
        totals = lax.psum(transposed_product(standard, projected), ("wide", "narrow"))
        inverse = invert_factor(gram_matrix)
        loadings_all = jnp.dot(totals, inverse.T, precision=lax.Precision.HIGHEST)
        if last_turn:
            loadings = lax.dynamic_slice_in_dim(loadings_all, position * share_rows, share_rows, 0)
        else:
            projected = jnp.dot(
                standard, loadings_all.astype(jnp.bfloat16), preferred_element_type=jnp.float32
            ).astype(jnp.bfloat16)
    scores = jnp.dot(
        projected.astype(jnp.float32), inverse.T, precision=lax.Precision.HIGHEST
    ) * math.sqrt(kept_total)
    return (scores, loadings)


def solution(mesh):
    in_specs = (P(("wide", "narrow"), None), P(("wide", "narrow")), P(), P())
    out_specs = (P(("wide", "narrow"), None), P("narrow", None))
    return jax.shard_map(
        on_device, mesh=mesh, in_specs=in_specs, out_specs=out_specs, check_vma=False
    )
```

profile of v0, /device:TPU:32, one launch (start us, length us, event | category | flops | bytes accessed | tf_op | source)
XLA Modules:
  0.0 639.3 jit_solution(8097715273102711557)
XLA Ops:
  7.2 0.8 compare_select_fusion
  8.0 0.7 compare_and_fusion
  8.7 0.7 convert_multiply_fusion
  9.4 19.5 %gather_fusion = bf16[896,4096]{1,0:T(8,128)(2,1)} fusion(bf16[1024,4096]{1,0:T(8,128)(2,1)} %param.7, s32[1024]{0:T(1024)S(1)} %pad_clamp_fusion), kind=kCustom, calls=%fused_computation | custom fusion | bytes 14683648 | tf_op jit(solution)/shard_map/jit(_take)/gather | solution.py:34
  28.9 6.6 %divide_convert_fusion = bf16[896,4096]{1,0:T(8,128)(2,1)S(1)} fusion(f32[4096]{0:T(1024)S(1)} %get-tuple-element.9, f32[4096]{0:T(1024)S(1)} %get-tuple-element.8, bf16[896,4096]{1,0:T(8,128)(2,1)} %gather_fusion, pred[896]{0:T(1024)(128)(4,1)S(1)} %compare_and_fusion), kind=kLoop, calls=%fused_computation.1 | loop fusion | flops 18350080 | bytes 14713728 | tf_op jit(solution)/shard_map/convert_element_type | solution.py:35
  35.5 2.1 convolution_convert_fusion.2
  37.6 3.5 fusion.10
  41.1 0.9 fusion.11
  42.0 0.2 all-reduce.5.cloned.1.call-start
  42.3 262.2 %all-reduce.7.cloned.1.call-done = (f32[4096,128]{1,0:T(8,128)}, f32[128,128]{0,1:T(8,128)}) async-done(((f32[4096,128]{1,0:T(8,128)}, f32[128,128]{0,1:T(8,128)}), (f32[4096,128]{1,0:T(8,128)}, f32[128,128]{0,1:T(8,128)})) %all-reduce.7.cloned.1.call-update) | async-done | bytes 2162704 | tf_op jit(solution)/shard_map/psum | solution.py:45
  304.4 0.9 copy.7
  305.4 0.9 fusion.9
  306.2 11.7 %cholesky.44 = f32[128,128]{1,0:T(8,128)S(1)} custom-call(f32[128,128]{1,0:T(8,128)S(1)} %fusion.9), custom_call_target="Cholesky" | custom-call | tf_op jit(solution)/shard_map/jit(cholesky)/cholesky | solution.py:18
  318.0 0.6 compare_reduce_fusion.1
  318.6 0.7 fusion.4
  319.3 9.8 %custom-call.6 = f32[1,128,128]{1,2,0:T(8,128)S(1)} custom-call(f32[1,128,128]{2,1,0:T(8,128)S(1)} %fusion.4), custom_call_target="InvertDiagBlocksLowerTriangular" | custom-call | tf_op jit(solution)/shard_map/jit(_solve_triangular)/triangular_solve | solution.py:20
  329.1 0.3 fusion.2
  329.4 3.5 convolution_convert_fusion
  333.0 5.3 convolution_convert_fusion.1
  338.3 3.5 fusion.13
  341.8 0.9 fusion.12
  342.7 259.1 %all-reduce.5.cloned.1.call-done = (f32[128,128]{0,1:T(8,128)}, f32[4096,128]{1,0:T(8,128)}) async-done(((f32[128,128]{0,1:T(8,128)}, f32[4096,128]{1,0:T(8,128)}), (f32[128,128]{0,1:T(8,128)}, f32[4096,128]{1,0:T(8,128)})) %all-reduce.5.cloned.1.call-update) | async-done | bytes 2162704 | tf_op jit(solution)/shard_map/psum | solution.py:44
  601.8 1.1 copy.9
  603.0 0.9 fusion.7
  603.8 11.7 %cholesky.55 = f32[128,128]{1,0:T(8,128)S(1)} custom-call(f32[128,128]{1,0:T(8,128)S(1)} %fusion.7), custom_call_target="Cholesky" | custom-call | tf_op jit(solution)/shard_map/jit(cholesky)/cholesky | solution.py:18
  615.6 0.6 compare_reduce_fusion
  616.2 0.7 fusion.5
  616.9 9.8 %custom-call.7 = f32[1,128,128]{1,2,0:T(8,128)S(1)} custom-call(f32[1,128,128]{2,1,0:T(8,128)S(1)} %fusion.5), custom_call_target="InvertDiagBlocksLowerTriangular" | custom-call | tf_op jit(solution)/shard_map/jit(_solve_triangular)/triangular_solve | solution.py:20
  626.7 0.3 fusion
  627.0 1.1 convolution_multiply_fusion
  628.1 3.5 fusion.14
  631.6 0.8 constant_dynamic-slice_fusion
  (15 shorter events, 0.2 us)
Async XLA Ops:
  7.2 28.3 %copy-start = (bf16[4096,128]{1,0:T(8,128)(2,1)S(1)}, bf16[4096,128]{1,0:T(8,128)(2,1)}, u32[]{:S(2)}) copy-start(bf16[4096,128]{1,0:T(8,128)(2,1)} %param.10) | copy-start | bytes 3145732
  7.2 297.3 %all-reduce.7.cloned.1.call-start = ((), (), s32[]{:S(2)}) async-start(), calls=%async_computation.1 | async-start | bytes 4325376 | tf_op jit(solution)/shard_map/psum | solution.py:45
  35.5 5.6 copy-start.1
  42.0 559.8 %all-reduce.5.cloned.1.call-start = ((), (), s32[]{:S(2)}) async-start(), calls=%async_computation | async-start | bytes 4325376 | tf_op jit(solution)/shard_map/psum | solution.py:44
  329.4 8.9 %slice-start = ((s8[7340032]{0:T(1024)(128)(4,1)}), s8[4194304]{0:T(1024)(128)(4,1)S(1)}, s32[]{:S(2)}) async-start(s8[7340032]{0:T(1024)(128)(4,1)} %bitcast.36), calls=%async_computation.2 | async-start | bytes 8388608
  332.9 5.3 slice-start.1
Sparse Core Ops, SparseCore 0:
  42.1 262.2 all-reduce.6
  342.8 258.9 all-reduce.4
where the time goes:
time: 643 us; the launch traced here: 639 us
  waiting for transfers between devices  521 us (81%)
  other arithmetic  56.2 us (9%)
  matrix products  24.9 us (4%)
  local copies, waits for them, and re-layouts  22.4 us (3%)
  between operations  14.2 us (2%)
    psum x1, waiting for transfers between devices, on_device(): lax.psum(transposed_product(standard, projected), ('wide', 'narrow'))  262 us
    psum x1, waiting for transfers between devices, on_device(): lax.psum(transposed_product(projected, projected), ('wide', 'narrow'))  259 us
    another operation x6, other arithmetic, invert_factor(): lower_factor = jnp.linalg.cholesky(gram_matrix)  24.8 us
    another operation x4, other arithmetic, invert_factor(): jax.scipy.linalg.solve_triangular(lower_factor, unit_matrix, lower=True)  20.9 us
    gather x1, local copies, waits for them, and re-layouts, on_device(): chosen = jnp.take(dosage, keep_rows, axis=0)  19.5 us
  transfers between devices with their start and end apart: 2, of which 2 were waited for; matrix products, arithmetic and copies ran while one was open for 0% of the time, Pallas kernels for 0%

commit v1 on v0

v1 whole, which is shorter than its diff:
```python
import functools
import itertools
import math

import jax
import jax.numpy as jnp
from jax import lax
from jax.experimental import pallas as pl
from jax.experimental.pallas import tpu as pltpu
from jax.sharding import PartitionSpec as P

X, Y, Z, C = 4, 4, 8, 2
LANES = 128
SNP_GROUP = 4 * LANES
ROW_CHUNK = 256
LANE_CHUNK = 1024
PIVOTS = 4
ITERS = 2
MESH = pl.DeviceIdType.MESH
HIGHEST = lax.Precision.HIGHEST
F32 = jnp.float32
BF16 = jnp.bfloat16


def device_at(x, y, z, c):
    return ((x * Z + z) * C + c, y)


def iota(shape, dim):
    return lax.broadcasted_iota(jnp.int32, shape, dim)


def dot_t(left, right, precision=None):
    return lax.dot_general(
        left, right, (((1,), (1,)), ((), ())), precision=precision, preferred_element_type=F32
    )


def eliminate(work, first, last):
    n = work.shape[0]
    row = iota((n, 1), 0)
    lane = iota((n, n), 1)
    lane1 = iota((1, n), 1)

    def panel(step, carry):
        k = step * PIVOTS
        whole = work[...]
        rows = [work[pl.ds(k + i, 1), :] for i in range(PIVOTS)]
        entry = {
            (i, l): jnp.sum(jnp.where(lane1 == k + l, rows[i], 0.0), axis=1, keepdims=True)
            for i in range(PIVOTS)
            for l in range(i, PIVOTS)
        }
        columns = [
            jnp.sum(jnp.where(lane == k + l, whole, 0.0), axis=1, keepdims=True)
            for l in range(PIVOTS)
        ]
        total = jnp.where((lane >= k) & (lane < k + PIVOTS) & (row >= k + PIVOTS), 0.0, whole)
        factors = []
        for j in range(PIVOTS):
            turn = 1.0 / entry[j, j]
            factor = jnp.where(row > k + j, columns[j] * turn, 0.0)
            factors.append(factor)
            own = jnp.where(lane1 == k + j, 1.0, rows[j])
            for l in range(j + 1, PIVOTS):
                columns[l] = columns[l] - factor * entry[j, l]
                less = entry[j, l] * turn
                rows[l] = jnp.where(lane1 == k + j, 0.0, rows[l]) - less * own
                for later in range(l, PIVOTS):
                    entry[l, later] = entry[l, later] - less * entry[j, later]
        for j in range(PIVOTS):
            own = jnp.where(lane1 == k + j, 1.0, rows[j])
            own = jnp.where((lane1 > k + j) & (lane1 < k + PIVOTS), 0.0, own)
            total = total - factors[j] * own
        work[...] = total
        for j in range(PIVOTS):
            work[pl.ds(k + j, 1), :] = rows[j]
        return carry

    lax.fori_loop(first, last, panel, 0)


def finish_inverse(work):
    n = work.shape[0]
    whole = work[...]
    row, lane = iota((n, n), 0), iota((n, n), 1)
    pivot = jnp.sum(jnp.where(row == lane, whole, 0.0), axis=1, keepdims=True)
    unit = jnp.where(lane < row, whole, jnp.where(lane == row, 1.0, 0.0))
    return unit * (1.0 / jnp.sqrt(pivot))


def kernel(
    samples_total, kept_total,
    dose_ref, keep_ref, counts_ref, sketch_ref,
    scores_ref, loads_ref,
    std, center, scale, mask, proj, proj_t, acc, gram, inverse,
    tot, rxc, own, rx1a, rx1b, rx2a, rx2b, zsrc, rxz, fin, fin2,
    g_src, g_core, g_half, g_rx, g_y, g_z, g_x, g_full,
    load_sem, send_sem, recv_sem,
):
    wide = lax.axis_index("wide")
    y = lax.axis_index("narrow")
    x, z, c = wide // (Z * C), lax.rem(wide // C, Z), lax.rem(wide, C)
    d = 1 - c
    xs = [lax.rem(x + k, X) for k in range(X)]
    ys = [lax.rem(y + k, Y) for k in range(Y)]
    zs = [lax.rem(z + k, Z) for k in range(Z)]
    core_peer = device_at(x, y, z, d)
    x_peer = [device_at(v, y, z, c) for v in xs]
    y_peer = [device_at(x, v, z, c) for v in ys]
    z_peer = [device_at(x, y, v, c) for v in zs]
    chunks = std.shape[0] // ROW_CHUNK
    snps = std.shape[1]

    def load(r):
        rows = pl.ds(r * ROW_CHUNK, ROW_CHUNK)
        return pltpu.make_async_copy(dose_ref.at[rows], std.at[rows], load_sem.at[r])

    for r in range(chunks):
        load(r).start()
    barrier = pltpu.get_barrier_semaphore()
    others = [core_peer] + x_peer[1:] + y_peer[1:] + z_peer[1:]
    for other in others:
        pl.semaphore_signal(barrier, inc=1, device_id=other, device_id_type=MESH)

    counter = itertools.count()
    sends = []

    def describe(src, dst, sem, peer):
        return pltpu.make_async_remote_copy(
            src_ref=src, dst_ref=dst, send_sem=send_sem.at[sem], recv_sem=recv_sem.at[sem],
            device_id=peer, device_id_type=MESH,
        )

    def push(src, dst, peer):
        copy = describe(src, dst, next(counter), peer)
        copy.start()
        sends.append(copy)
        return copy

    frequency = counts_ref[...].astype(F32) / (2.0 * samples_total)
    center[...] = 2.0 * frequency
    scale[...] = 1.0 / jnp.sqrt(2.0 * frequency * (1.0 - frequency))
    keep_count = keep_ref.shape[1]
    ones = jnp.ones((keep_count, LANES), BF16)

    def mark(r, carry):
        hits = iota((ROW_CHUNK, keep_count), 0) + r * ROW_CHUNK == keep_ref[...]
        mask[pl.ds(pl.multiple_of(r * ROW_CHUNK, ROW_CHUNK), ROW_CHUNK), :] = jnp.dot(
            jnp.where(hits, 1.0, 0.0).astype(BF16), ones, preferred_element_type=F32
        )
        return carry

    lax.fori_loop(0, chunks, mark, 0)

    def keep_projection(r, value):
        rows = pl.ds(pl.multiple_of(r * ROW_CHUNK, ROW_CHUNK), ROW_CHUNK)
        value = value.astype(BF16).astype(F32) * mask[rows, :]
        proj[rows, :] = value.astype(BF16)
        proj_t[:, rows] = value.T.astype(BF16)

    def first_projection(r, carry):
        load(r).wait()
        rows = pl.ds(pl.multiple_of(r * ROW_CHUNK, ROW_CHUNK), ROW_CHUNK)
        value = jnp.zeros((ROW_CHUNK, LANES), F32)
        for q in range(snps // LANE_CHUNK):
            lanes = pl.ds(q * LANE_CHUNK, LANE_CHUNK)
            part = ((std[rows, lanes].astype(F32) - center[:, lanes]) * scale[:, lanes]).astype(BF16)
            std[rows, lanes] = part
            value = value + jnp.dot(part, sketch_ref[lanes, :], preferred_element_type=F32)
        keep_projection(r, value)
        return carry

    lax.fori_loop(0, chunks, first_projection, 0)

    def group_lanes(yy, cc):
        return pl.ds(pl.multiple_of((yy * C + cc) * SNP_GROUP, SNP_GROUP), SNP_GROUP)

    def partial_group(yy, cc):
        value = jnp.dot(proj_t[...], std[:, group_lanes(yy, cc)], preferred_element_type=F32)
        for q in range(X):
            tot[yy, cc, q] = value[:, q * LANES:(q + 1) * LANES].reshape(8, 16, LANES)

    for it in range(ITERS):
        last = it + 1 == ITERS
        g_src[it] = dot_t(proj_t[...], proj_t[...]).reshape(C, X, 16, LANES)
        if it == 0:
            pl.semaphore_wait(barrier, len(others))
        gram_core = push(g_src.at[it, d], g_core.at[it], core_peer)

        core_sem = next(counter)
        for _ in range(Y - 1):
            next(counter)

        def core_copy(j, it=it, core_sem=core_sem):
            yy = lax.rem(y + 1 + j, Y)
            return describe(tot.at[yy, d], rxc.at[it, yy], core_sem + j, core_peer)

        def partial_other(j, carry):
            partial_group(lax.rem(y + 1 + j, Y), d)
            core_copy(j).start()
            return carry

        def partial_own(j, carry):
            partial_group(lax.rem(y + 1 + j, Y), c)
            return carry

        lax.fori_loop(0, Y, partial_other, 0)
        gram_core.wait_recv()
        g_half[it] = g_src[it, c] + g_core[it]
        gram_x = [push(g_half.at[it, xs[k]], g_rx.at[it, k - 1], x_peer[k]) for k in range(1, X)]
        lax.fori_loop(0, Y, partial_own, 0)
        for copy in gram_x:
            copy.wait_recv()
        g_y[it, y] = g_half[it, x] + g_rx[it, 0] + g_rx[it, 1] + g_rx[it, 2]
        gram_y = [push(g_y.at[it, y], g_y.at[it, y], y_peer[k]) for k in range(1, Y)]

        first_a, first_b = {}, {}
        for j in (1, 2, 3, 0):
            core_copy((j + 3) % 4).wait_recv()
            yy = ys[j]
            own[it, yy] = tot[yy, c] + rxc[it, yy]
            for k in range(1, X):
                first_a[j, k] = push(
                    own.at[it, yy, xs[k], pl.ds(0, 4)], rx1a.at[it, k - 1, yy], x_peer[k]
                )
            if j:
                for k in (1, 2, 3, 0):
                    first_b[k, j] = push(
                        own.at[it, yy, xs[k], pl.ds(4, 4)], rx1b.at[it, j - 1, xs[k]], y_peer[j]
                    )
        for copy in gram_y:
            copy.wait_recv()
        g_z[it, z] = (g_y[it, 0] + g_y[it, 1]) + (g_y[it, 2] + g_y[it, 3])
        gram_z = [push(g_z.at[it, z], g_z.at[it, z], z_peer[k]) for k in range(1, Z)]

        second_a, second_b = [], []
        for j in (1, 2, 3, 0):
            for k in range(1, X):
                first_a[j, k].wait_recv()
            own[it, ys[j], x, 0:4] = (
                own[it, ys[j], x, 0:4] + rx1a[it, 0, ys[j]] + rx1a[it, 1, ys[j]] + rx1a[it, 2, ys[j]]
            )
            if j:
                second_a.append(push(own.at[it, ys[j], x, pl.ds(0, 4)], rx2a.at[it, j - 1], y_peer[j]))
            for k in range(1, Y):
                first_b[j, k].wait_recv()
            own[it, y, xs[j], 4:8] = (
                own[it, y, xs[j], 4:8] + rx1b[it, 0, xs[j]] + rx1b[it, 1, xs[j]] + rx1b[it, 2, xs[j]]
            )
            if j:
                second_b.append(push(own.at[it, y, xs[j], pl.ds(4, 4)], rx2b.at[it, j - 1], x_peer[j]))
        for copy in gram_z:
            copy.wait_recv()
        value = g_z[it, 0]
        for k in range(1, Z):
            value = value + g_z[it, k]
        g_x[it, x] = value
        gram_x = [push(g_x.at[it, x], g_x.at[it, x], x_peer[k]) for k in range(1, X)]
        for copy in second_a + second_b:
            copy.wait_recv()
        zsrc[it, 0:4] = own[it, y, x, 0:4] + rx2a[it, 0] + rx2a[it, 1] + rx2a[it, 2]
        zsrc[it, 4:8] = own[it, y, x, 4:8] + rx2b[it, 0] + rx2b[it, 1] + rx2b[it, 2]
        third = [push(zsrc.at[it, zs[k]], rxz.at[it, k - 1], z_peer[k]) for k in range(1, Z)]
        for copy in gram_x:
            copy.wait_recv()
        g_full[it, c] = g_x[it]
        gram_core = push(g_full.at[it, c], g_full.at[it, c], core_peer)
        for copy in third:
            copy.wait_recv()
        value = zsrc[it, z]
        for k in range(1, Z):
            value = value + rxz[it, k - 1]
        if last:
            mine = fin2.at[c, x]
        else:
            mine = fin.at[y, c, x]
        mine[z] = value
        gather_z = [push(mine.at[z], mine.at[z], z_peer[k]) for k in range(1, Z)]
        gram_core.wait_recv()
        gram[...] = g_full[it].reshape(LANES, LANES)
        panels = LANES // PIVOTS
        eliminate(gram, 0, 12)
        for copy in gather_z:
            copy.wait_recv()
        if last:
            gather_x = [push(mine, mine, x_peer[k]) for k in range(1, X)]
            gather_c = [push(mine, mine, core_peer)]
            eliminate(gram, 12, 20)
            for k in range(1, X):
                gather_x[k - 1].wait_recv()
                block = fin2.at[c, xs[X - k]]
                gather_c.append(push(block, block, core_peer))
            eliminate(gram, 20, panels)
            inverse[...] = finish_inverse(gram)
            keep_column = jnp.broadcast_to(keep_ref[...].astype(F32), (LANES, keep_count)).T
            value = jnp.zeros((keep_count, LANES), F32)
            for q in range(std.shape[0] // LANES):
                hits = keep_column == (iota((keep_count, LANES), 1) + q * LANES).astype(F32)
                value = value + jnp.dot(
                    jnp.where(hits, 1.0, 0.0).astype(BF16), proj[q * LANES:(q + 1) * LANES, :],
                    preferred_element_type=F32,
                )
            scores_ref[...] = dot_t(value, inverse[...], HIGHEST) * math.sqrt(kept_total)
            for copy in gather_c:
                copy.wait_recv()
            for cc in range(C):
                for q in range(X):
                    value = jnp.dot(
                        inverse[...], fin2[cc, q].reshape(LANES, LANES), precision=HIGHEST,
                        preferred_element_type=F32,
                    )
                    loads_ref[(cc * X + q) * LANES:(cc * X + q + 1) * LANES, :] = value.T
        else:
            gather_x = [push(mine, mine, x_peer[k]) for k in range(1, X)]
            gather_y = [push(mine, mine, y_peer[k]) for k in range(1, Y)]
            gather_c = [push(mine, mine, core_peer)]
            eliminate(gram, 12, 20)
            corner_a, corner_b = {}, {}
            for j in range(1, Y):
                gather_y[j - 1].wait_recv()
                block = fin.at[ys[Y - j], c, x]
                for k in range(1, X):
                    corner_a[j, k] = push(block.at[pl.ds(0, 4)], block.at[pl.ds(0, 4)], x_peer[k])
                gather_x[j - 1].wait_recv()
                block2 = fin.at[y, c, xs[X - j]]
                for k in range(1, Y):
                    corner_b[j, k] = push(block2.at[pl.ds(4, 4)], block2.at[pl.ds(4, 4)], y_peer[k])
                gather_c.append(push(block, block, core_peer))
                gather_c.append(push(block2, block2, core_peer))
            eliminate(gram, 20, panels)
            inverse[...] = finish_inverse(gram)
            for j in range(1, Y):
                for k in range(1, X):
                    corner_a[j, k].wait_recv()
                    corner_b[k, j].wait_recv()
                    block = fin.at[ys[Y - j], c, xs[X - k]]
                    gather_c.append(push(block, block, core_peer))

            def apply_group(yy, cc):
                value = jnp.concatenate([fin[yy, cc, q].reshape(LANES, LANES) for q in range(X)], axis=1)
                value = jnp.dot(inverse[...], value, precision=HIGHEST, preferred_element_type=F32)
                return dot_t(std[:, group_lanes(yy, cc)], value.astype(BF16))

            def project_own(j, carry):
                acc[...] = acc[...] + apply_group(lax.rem(y + j, Y), c)
                return carry

            def project_other(j, carry):
                acc[...] = acc[...] + apply_group(lax.rem(y + j, Y), d)
                return carry

            acc[...] = jnp.zeros_like(acc)
            lax.fori_loop(0, Y, project_own, 0)
            for copy in gather_c:
                copy.wait_recv()
            lax.fori_loop(0, Y, project_other, 0)

            def keep_chunk(r, carry):
                rows = pl.ds(pl.multiple_of(r * ROW_CHUNK, ROW_CHUNK), ROW_CHUNK)
                keep_projection(r, acc[rows, :])
                return carry

            lax.fori_loop(0, chunks, keep_chunk, 0)
        for j in range(Y):
            core_copy(j).wait_send()
    for copy in sends:
        copy.wait_send()


def on_device(dosage, keep_rows, allele_counts, projection):
    groups = lax.axis_size("wide") * lax.axis_size("narrow")
    samples, snps = dosage.shape
    kept = keep_rows.shape[0]
    shares = snps // Y
    vmem = pl.BlockSpec(memory_space=pltpu.VMEM)
    piece = (4, 16, LANES)
    block = (8, 16, LANES)
    scratch = [
        ((samples, snps), BF16),
        ((1, snps), F32),
        ((1, snps), F32),
        ((samples, LANES), F32),
        ((samples, LANES), BF16),
        ((LANES, samples), BF16),
        ((samples, LANES), F32),
        ((LANES, LANES), F32),
        ((LANES, LANES), F32),
        ((Y, C, X) + block, F32),
        ((ITERS, Y, X) + block, F32),
        ((ITERS, Y, X) + block, F32),
        ((ITERS, X - 1, Y) + piece, F32),
        ((ITERS, Y - 1, X) + piece, F32),
        ((ITERS, Y - 1) + piece, F32),
        ((ITERS, X - 1) + piece, F32),
        ((ITERS,) + block, F32),
        ((ITERS, Z - 1, 16, LANES), F32),
        ((Y, C, X) + block, F32),
        ((C, X) + block, F32),
        ((ITERS, C, X, 16, LANES), F32),
        ((ITERS, X, 16, LANES), F32),
        ((ITERS, X, 16, LANES), F32),
        ((ITERS, X - 1, 16, LANES), F32),
        ((ITERS, Y, 16, LANES), F32),
        ((ITERS, Z, 16, LANES), F32),
        ((ITERS, X, 16, LANES), F32),
        ((ITERS, C, X, 16, LANES), F32),
    ]
    return pl.pallas_call(
        functools.partial(kernel, samples * groups, kept * groups),
        name="subspace",
        out_shape=(
            jax.ShapeDtypeStruct((kept, LANES), F32),
            jax.ShapeDtypeStruct((shares, LANES), F32),
        ),
        in_specs=[pl.BlockSpec(memory_space=pl.ANY), vmem, vmem, vmem],
        out_specs=(vmem, vmem),
        scratch_shapes=[pltpu.VMEM(shape, kind) for shape, kind in scratch]
        + [
            pltpu.SemaphoreType.DMA((samples // ROW_CHUNK,)),
            pltpu.SemaphoreType.DMA((200,)),
            pltpu.SemaphoreType.DMA((200,)),
        ],
        compiler_params=pltpu.CompilerParams(
            collective_id=0, has_side_effects=True, vmem_limit_bytes=56 * 2**20
        ),
        cost_estimate=pl.CostEstimate(flops=4_500_000_000, bytes_accessed=12_000_000, transcendentals=0),
    )(dosage, keep_rows.reshape(1, kept), allele_counts.reshape(1, snps), projection)


def solution(mesh):
    in_specs = (P(("wide", "narrow"), None), P(("wide", "narrow")), P(), P())
    out_specs = (P(("wide", "narrow"), None), P("narrow", None))
    return jax.shard_map(
        on_device, mesh=mesh, in_specs=in_specs, out_specs=out_specs, check_vma=False
    )
```

time: 643 us -> 101 us (0.16)
  waiting for transfers between devices: 521 us -> 0 us
  Pallas kernels: 0 us -> 94.9 us
  other arithmetic: 56.2 us -> 0 us
  matrix products: 24.9 us -> 0 us
  local copies, waits for them, and re-layouts: 22.4 us -> 4.95 us
  between operations: 14.2 us -> 0.64 us
    psum x2 -> x0, waiting for transfers between devices: 521 us -> none  [the longest x1 262 us: on_device(): lax.psum(transposed_product(standard, projected), ('wide', 'narrow'))]
    pallas_call x0 -> x1, Pallas kernels: none -> 94.9 us  [on_device(): pl.pallas_call(functools.partial(kernel, samples * groups, kept * groups)...]
    another operation x10 -> x0, other arithmetic: 45.7 us -> none  [the longest x6 24.8 us: invert_factor(): lower_factor = jnp.linalg.cholesky(gram_matrix)]
    dot_general x9 -> x0, matrix products: 24.3 us -> none  [the longest x4 8.84 us: transposed_product(): lax.dot_general(left_side, right_side, (((0,), (0,)), ((), ())), preferre...]
    gather x1 -> x0, local copies, waits for them, and re-layouts: 19.5 us -> none  [on_device(): chosen = jnp.take(dosage, keep_rows, axis=0)]
    convert_element_type x1 -> x0, other arithmetic: 6.56 us -> none  [on_device(): ((chosen.astype(jnp.float32) - center) / spread).astype(jnp.bfloat16)]
  transfers between devices with their start and end apart: 2 -> 0, of which waited for: 2 -> 0; matrix products, arithmetic and copies ran while one was open for 0% -> 0% of each run, Pallas kernels for 0% -> 0%
where the time goes in v1:
time: 101 us; the launch traced here: 100 us
  Pallas kernels  94.9 us (94%)
  local copies, waits for them, and re-layouts  4.95 us (5%)
    pallas_call x1, Pallas kernels, on_device(): pl.pallas_call(functools.partial(kernel, samples * groups, kept * groups)...  94.9 us
    unnamed x2, local copies, waits for them, and re-layouts  3.68 us

profile of v1, /device:TPU:32, one launch (start us, length us, event | category | flops | bytes accessed | tf_op | source)
XLA Modules:
  0.0 100.5 jit_solution(4398088960360458915)
XLA Ops:
  0.6 1.3 %reshape.10.keep_ref = s32[1,896]{1,0:T(1,128)} reshape(s32[896]{0:T(1024)} %param.5) | data formatting | bytes 7168 | tf_op jit(solution)/shard_map/reshape | solution.py:428
  1.9 94.9 %subspace.1 = (f32[896,128]{1,0:T(8,128)}, f32[1024,128]{1,0:T(8,128)}) custom-call(bf16[1024,4096]{1,0:T(8,128)(2,1)} %dose_ref.1, s32[1,896]{1,0:T(1,128)} %reshape.10.keep_ref, s32[1,4096]{1,0:T(1,128)} %bitcast.1, bf16[4096,128]{1,0:T(8,128)(2,1)} %sketch_ref.1), custom_call_target="tpu_custom_call" | custom-call | flops 4499999744 | bytes 12000000 | tf_op jit(solution)/shard_map/subspace/pallas_call | solution.py:409
  96.8 1.8 %copy.8 = f32[896,128]{1,0:T(8,128)} copy(f32[896,128]{1,0:T(8,128)} %get-tuple-element.4) | data formatting | bytes 917504
  98.6 1.9 %copy.9 = f32[1024,128]{1,0:T(8,128)} copy(f32[1024,128]{1,0:T(8,128)} %get-tuple-element.5) | data formatting | bytes 1048576

commit v2 on v1

--- a/solution.py
+++ b/solution.py
@@ -13,9 +13,11 @@
 LANES = 128
 SNP_GROUP = 4 * LANES
 ROW_CHUNK = 256
+HALF_ROWS = 512
 LANE_CHUNK = 1024
 PIVOTS = 4
 ITERS = 2
+PARTS = 2
 MESH = pl.DeviceIdType.MESH
 HIGHEST = lax.Precision.HIGHEST
 F32 = jnp.float32
@@ -89,14 +91,33 @@
     return unit * (1.0 / jnp.sqrt(pivot))
 
 
+def hand_on(scores_in, loads_in, scores_out, loads_out, scores, loads, sem):
+    parts = []
+    for source, held, target in ((scores_in, scores, scores_out), (loads_in, loads, loads_out)):
+        size = source.shape[0] // PARTS
+        for q in range(PARTS):
+            rows, n = pl.ds(q * size, size), len(parts)
+            parts.append((
+                pltpu.make_async_copy(source.at[rows], held.at[rows], sem.at[n]),
+                pltpu.make_async_copy(held.at[rows], target.at[rows], sem.at[n + 2 * PARTS]),
+            ))
+    for read, _ in parts:
+        read.start()
+    for read, write in parts:
+        read.wait()
+        write.start()
+    for _, write in parts:
+        write.wait()
+
+
 def kernel(
-    samples_total, kept_total,
+    samples_total, root,
     dose_ref, keep_ref, counts_ref, sketch_ref,
     scores_ref, loads_ref,
-    std, center, scale, mask, proj, proj_t, acc, gram, inverse,
+    std, sketch, center, scale, mask, proj, proj_t, acc, gram, inverse, basis_t, scores, loads, kept_proj,
     tot, rxc, own, rx1a, rx1b, rx2a, rx2b, zsrc, rxz, fin, fin2,
     g_src, g_core, g_half, g_rx, g_y, g_z, g_x, g_full,
-    load_sem, send_sem, recv_sem,
+    load_sem, sketch_sem, out_sem, send_sem, recv_sem,
 ):
     wide = lax.axis_index("wide")
     y = lax.axis_index("narrow")
@@ -116,6 +137,8 @@
         rows = pl.ds(r * ROW_CHUNK, ROW_CHUNK)
         return pltpu.make_async_copy(dose_ref.at[rows], std.at[rows], load_sem.at[r])
 
+    sketch_load = pltpu.make_async_copy(sketch_ref, sketch, sketch_sem)
+    sketch_load.start()
     for r in range(chunks):
         load(r).start()
     barrier = pltpu.get_barrier_semaphore()
@@ -141,11 +164,12 @@
     frequency = counts_ref[...].astype(F32) / (2.0 * samples_total)
     center[...] = 2.0 * frequency
     scale[...] = 1.0 / jnp.sqrt(2.0 * frequency * (1.0 - frequency))
-    keep_count = keep_ref.shape[1]
+    keep_row = jnp.concatenate([keep_ref[q:q + 1, :] for q in range(keep_ref.shape[0])], axis=1)
+    keep_count = keep_row.shape[1]
     ones = jnp.ones((keep_count, LANES), BF16)
 
     def mark(r, carry):
-        hits = iota((ROW_CHUNK, keep_count), 0) + r * ROW_CHUNK == keep_ref[...]
+        hits = iota((ROW_CHUNK, keep_count), 0) + r * ROW_CHUNK == keep_row
         mask[pl.ds(pl.multiple_of(r * ROW_CHUNK, ROW_CHUNK), ROW_CHUNK), :] = jnp.dot(
             jnp.where(hits, 1.0, 0.0).astype(BF16), ones, preferred_element_type=F32
         )
@@ -167,10 +191,11 @@
             lanes = pl.ds(q * LANE_CHUNK, LANE_CHUNK)
             part = ((std[rows, lanes].astype(F32) - center[:, lanes]) * scale[:, lanes]).astype(BF16)
             std[rows, lanes] = part
-            value = value + jnp.dot(part, sketch_ref[lanes, :], preferred_element_type=F32)
+            value = value + jnp.dot(part, sketch[lanes, :], preferred_element_type=F32)
         keep_projection(r, value)
         return carry
 
+    sketch_load.wait()
     lax.fori_loop(0, chunks, first_projection, 0)
 
     def group_lanes(yy, cc):
@@ -205,10 +230,11 @@
             partial_group(lax.rem(y + 1 + j, Y), c)
             return carry
 
-        lax.fori_loop(0, Y, partial_other, 0)
+        lax.fori_loop(0, 2, partial_other, 0)
         gram_core.wait_recv()
         g_half[it] = g_src[it, c] + g_core[it]
         gram_x = [push(g_half.at[it, xs[k]], g_rx.at[it, k - 1], x_peer[k]) for k in range(1, X)]
+        lax.fori_loop(2, Y, partial_other, 0)
         lax.fori_loop(0, Y, partial_own, 0)
         for copy in gram_x:
             copy.wait_recv()
@@ -229,6 +255,16 @@
                     first_b[k, j] = push(
                         own.at[it, yy, xs[k], pl.ds(4, 4)], rx1b.at[it, j - 1, xs[k]], y_peer[j]
                     )
+        if last:
+            keep_column = jnp.broadcast_to(keep_row.astype(F32), (LANES, keep_count)).T
+            value = jnp.zeros((keep_count, LANES), F32)
+            for q in range(std.shape[0] // LANES):
+                hits = keep_column == (iota((keep_count, LANES), 1) + q * LANES).astype(F32)
+                value = value + jnp.dot(
+                    jnp.where(hits, 1.0, 0.0).astype(BF16), proj[q * LANES:(q + 1) * LANES, :],
+                    preferred_element_type=F32,
+                )
+            kept_proj[...] = value
         for copy in gram_y:
             copy.wait_recv()
         g_z[it, z] = (g_y[it, 0] + g_y[it, 1]) + (g_y[it, 2] + g_y[it, 3])
@@ -280,81 +316,101 @@
         gram_core.wait_recv()
         gram[...] = g_full[it].reshape(LANES, LANES)
         panels = LANES // PIVOTS
-        eliminate(gram, 0, 12)
+        eliminate(gram, 0, 20)
         for copy in gather_z:
             copy.wait_recv()
         if last:
             gather_x = [push(mine, mine, x_peer[k]) for k in range(1, X)]
             gather_c = [push(mine, mine, core_peer)]
-            eliminate(gram, 12, 20)
             for k in range(1, X):
                 gather_x[k - 1].wait_recv()
                 block = fin2.at[c, xs[X - k]]
                 gather_c.append(push(block, block, core_peer))
             eliminate(gram, 20, panels)
             inverse[...] = finish_inverse(gram)
-            keep_column = jnp.broadcast_to(keep_ref[...].astype(F32), (LANES, keep_count)).T
-            value = jnp.zeros((keep_count, LANES), F32)
-            for q in range(std.shape[0] // LANES):
-                hits = keep_column == (iota((keep_count, LANES), 1) + q * LANES).astype(F32)
-                value = value + jnp.dot(
-                    jnp.where(hits, 1.0, 0.0).astype(BF16), proj[q * LANES:(q + 1) * LANES, :],
-                    preferred_element_type=F32,
-                )
-            scores_ref[...] = dot_t(value, inverse[...], HIGHEST) * math.sqrt(kept_total)
+            scores[...] = dot_t(kept_proj[...], inverse[...], HIGHEST) * root
+            results = [pltpu.make_async_copy(scores, scores_ref, out_sem.at[0])]
+            results[0].start()
+
+            def load_half(cc, place):
+                value = jnp.concatenate([fin2[cc, q].reshape(LANES, LANES) for q in range(X)], axis=1)
+                value = jnp.dot(inverse[...], value, precision=HIGHEST, preferred_element_type=F32)
+                rows = pl.ds(pl.multiple_of(cc * SNP_GROUP, SNP_GROUP), SNP_GROUP)
+                loads[rows, :] = value.T
+                copy = pltpu.make_async_copy(loads.at[rows], loads_ref.at[rows], out_sem.at[place])
+                copy.start()
+                results.append(copy)
+
+            load_half(c, 1)
             for copy in gather_c:
                 copy.wait_recv()
-            for cc in range(C):
-                for q in range(X):
-                    value = jnp.dot(
-                        inverse[...], fin2[cc, q].reshape(LANES, LANES), precision=HIGHEST,
-                        preferred_element_type=F32,
-                    )
-                    loads_ref[(cc * X + q) * LANES:(cc * X + q + 1) * LANES, :] = value.T
+            load_half(d, 2)
+            for copy in results:
+                copy.wait()
         else:
-            gather_x = [push(mine, mine, x_peer[k]) for k in range(1, X)]
-            gather_y = [push(mine, mine, y_peer[k]) for k in range(1, Y)]
+            half_a, half_b = pl.ds(0, 4), pl.ds(4, 4)
+
+            def pass_on(block, half, peer):
+                return push(block.at[half], block.at[half], peer)
+
+            near_a = [pass_on(mine, half_a, y_peer[k]) for k in range(1, Y)]
+            near_b = [pass_on(mine, half_b, x_peer[k]) for k in range(1, X)]
+            late_a = [pass_on(mine, half_a, x_peer[k]) for k in range(1, X)]
+            late_b = [pass_on(mine, half_b, y_peer[k]) for k in range(1, Y)]
             gather_c = [push(mine, mine, core_peer)]
-            eliminate(gram, 12, 20)
+            eliminate(gram, 20, panels)
+            inverse[...] = finish_inverse(gram)
             corner_a, corner_b = {}, {}
             for j in range(1, Y):
-                gather_y[j - 1].wait_recv()
+                near_a[j - 1].wait_recv()
+                for k in range(1, X):
+                    corner_a[j, k] = pass_on(fin.at[ys[Y - j], c, x], half_a, x_peer[k])
+                near_b[j - 1].wait_recv()
+                for k in range(1, Y):
+                    corner_b[j, k] = pass_on(fin.at[y, c, xs[X - j]], half_b, y_peer[k])
+            acc[...] = jnp.zeros_like(acc)
+
+            def add_group(yy, cc):
+                value = jnp.concatenate([fin[yy, cc, q].reshape(LANES, LANES) for q in range(X)], axis=1)
+                value = jnp.dot(inverse[...], value, precision=HIGHEST, preferred_element_type=F32)
+                basis_t[...] = value.astype(BF16)
+
+                def add_rows(r, carry):
+                    rows = pl.ds(pl.multiple_of(r * HALF_ROWS, HALF_ROWS), HALF_ROWS)
+                    acc[rows, :] = acc[rows, :] + dot_t(std[rows, group_lanes(yy, cc)], basis_t[...])
+                    return carry
+
+                lax.fori_loop(0, std.shape[0] // HALF_ROWS, add_rows, 0)
+
+            same_y = [gather_c[0]]
+            for j in range(1, X):
+                late_a[j - 1].wait_recv()
+                block = fin.at[y, c, xs[X - j]]
+                same_y.append(push(block, block, core_peer))
+            other_y = []
+            for j in range(1, Y):
+                late_b[j - 1].wait_recv()
                 block = fin.at[ys[Y - j], c, x]
-                for k in range(1, X):
-                    corner_a[j, k] = push(block.at[pl.ds(0, 4)], block.at[pl.ds(0, 4)], x_peer[k])
-                gather_x[j - 1].wait_recv()
-                block2 = fin.at[y, c, xs[X - j]]
-                for k in range(1, Y):
-                    corner_b[j, k] = push(block2.at[pl.ds(4, 4)], block2.at[pl.ds(4, 4)], y_peer[k])
-                gather_c.append(push(block, block, core_peer))
-                gather_c.append(push(block2, block2, core_peer))
-            eliminate(gram, 20, panels)
-            inverse[...] = finish_inverse(gram)
+                other_y.append(push(block, block, core_peer))
+            add_group(y, c)
+            for copy in same_y:
+                copy.wait_recv()
+            add_group(y, d)
             for j in range(1, Y):
                 for k in range(1, X):
                     corner_a[j, k].wait_recv()
                     corner_b[k, j].wait_recv()
                     block = fin.at[ys[Y - j], c, xs[X - k]]
-                    gather_c.append(push(block, block, core_peer))
-
-            def apply_group(yy, cc):
-                value = jnp.concatenate([fin[yy, cc, q].reshape(LANES, LANES) for q in range(X)], axis=1)
-                value = jnp.dot(inverse[...], value, precision=HIGHEST, preferred_element_type=F32)
-                return dot_t(std[:, group_lanes(yy, cc)], value.astype(BF16))
-
-            def project_own(j, carry):
-                acc[...] = acc[...] + apply_group(lax.rem(y + j, Y), c)
+                    other_y.append(push(block, block, core_peer))
+                add_group(ys[Y - j], c)
+            for copy in other_y:
+                copy.wait_recv()
+
+            def add_other(j, carry):
+                add_group(lax.rem(y + j, Y), d)
                 return carry
 
-            def project_other(j, carry):
-                acc[...] = acc[...] + apply_group(lax.rem(y + j, Y), d)
-                return carry
-
-            acc[...] = jnp.zeros_like(acc)
-            lax.fori_loop(0, Y, project_own, 0)
-            for copy in gather_c:
-                copy.wait_recv()
-            lax.fori_loop(0, Y, project_other, 0)
+            lax.fori_loop(1, Y, add_other, 0)
 
             def keep_chunk(r, carry):
                 rows = pl.ds(pl.multiple_of(r * ROW_CHUNK, ROW_CHUNK), ROW_CHUNK)
@@ -378,6 +434,7 @@
     block = (8, 16, LANES)
     scratch = [
         ((samples, snps), BF16),
+        ((snps, LANES), BF16),
         ((1, snps), F32),
         ((1, snps), F32),
         ((samples, LANES), F32),
@@ -386,6 +443,10 @@
         ((samples, LANES), F32),
         ((LANES, LANES), F32),
         ((LANES, LANES), F32),
+        ((LANES, SNP_GROUP), BF16),
+        ((kept, LANES), F32),
+        ((shares, LANES), F32),
+        ((kept, LANES), F32),
         ((Y, C, X) + block, F32),
         ((ITERS, Y, X) + block, F32),
         ((ITERS, Y, X) + block, F32),
@@ -406,26 +467,44 @@
         ((ITERS, X, 16, LANES), F32),
         ((ITERS, C, X, 16, LANES), F32),
     ]
-    return pl.pallas_call(
-        functools.partial(kernel, samples * groups, kept * groups),
+    any_place = pl.BlockSpec(memory_space=pl.ANY)
+    results = (
+        jax.ShapeDtypeStruct((kept, LANES), F32),
+        jax.ShapeDtypeStruct((shares, LANES), F32),
+    )
+    computed = pl.pallas_call(
+        functools.partial(kernel, samples * groups, math.sqrt(kept * groups)),
         name="subspace",
-        out_shape=(
-            jax.ShapeDtypeStruct((kept, LANES), F32),
-            jax.ShapeDtypeStruct((shares, LANES), F32),
-        ),
-        in_specs=[pl.BlockSpec(memory_space=pl.ANY), vmem, vmem, vmem],
-        out_specs=(vmem, vmem),
+        out_shape=results,
+        in_specs=[any_place, vmem, vmem, any_place],
+        out_specs=(any_place, any_place),
         scratch_shapes=[pltpu.VMEM(shape, kind) for shape, kind in scratch]
         + [
             pltpu.SemaphoreType.DMA((samples // ROW_CHUNK,)),
-            pltpu.SemaphoreType.DMA((200,)),
-            pltpu.SemaphoreType.DMA((200,)),
+            pltpu.SemaphoreType.DMA,
+            pltpu.SemaphoreType.DMA((3,)),
+            pltpu.SemaphoreType.DMA((220,)),
+            pltpu.SemaphoreType.DMA((220,)),
         ],
         compiler_params=pltpu.CompilerParams(
             collective_id=0, has_side_effects=True, vmem_limit_bytes=56 * 2**20
         ),
         cost_estimate=pl.CostEstimate(flops=4_500_000_000, bytes_accessed=12_000_000, transcendentals=0),
-    )(dosage, keep_rows.reshape(1, kept), allele_counts.reshape(1, snps), projection)
+    )(dosage, keep_rows.reshape(kept // LANES, LANES), allele_counts.reshape(1, snps), projection)
+    return pl.pallas_call(
+        hand_on,
+        name="outputs",
+        out_shape=results,
+        in_specs=[any_place, any_place],
+        out_specs=(any_place, any_place),
+        scratch_shapes=[
+            pltpu.VMEM((kept, LANES), F32),
+            pltpu.VMEM((shares, LANES), F32),
+            pltpu.SemaphoreType.DMA((4 * PARTS,)),
+        ],
+        compiler_params=pltpu.CompilerParams(vmem_limit_bytes=56 * 2**20),
+        cost_estimate=pl.CostEstimate(flops=0, bytes_accessed=2_000_000, transcendentals=0),
+    )(*computed)
 
 
 def solution(mesh):

time: 101 us -> 96.6 us (0.956)
  local copies, waits for them, and re-layouts: 4.95 us -> 0 us
    unnamed x2 -> x0, local copies, waits for them, and re-layouts: 3.68 us -> none
    reshape x1 -> x0, local copies, waits for them, and re-layouts: 1.27 us -> none  [on_device(): keep_rows.reshape(1, kept)]
    pallas_call x1 -> x2, Pallas kernels: 94.9 us -> 95.3 us  [the longest x1 93.3 us: on_device(): pl.pallas_call(functools.partial(kernel, samples * groups, math.sqrt(kept...]
where the time goes in v2:
time: 96.6 us; the launch traced here: 96 us
  Pallas kernels  95.3 us (99%)
    pallas_call x1, Pallas kernels, on_device(): pl.pallas_call(functools.partial(kernel, samples * groups, math.sqrt(kept...  93.3 us
    pallas_call x1, Pallas kernels, on_device(): pl.pallas_call(hand_on, name='outputs', out_shape=results, in_specs=[any_...  2.04 us

profile of v2, /device:TPU:32, one launch (start us, length us, event | category | flops | bytes accessed | tf_op | source)
XLA Modules:
  0.0 96.0 jit_solution(1021431950361592252)
XLA Ops:
  0.6 93.3 %subspace.1 = (f32[896,128]{1,0:T(8,128)}, f32[1024,128]{1,0:T(8,128)}) custom-call(bf16[1024,4096]{1,0:T(8,128)(2,1)} %dose_ref.1, s32[7,128]{1,0:T(8,128)} %bitcast.3, s32[1,4096]{1,0:T(1,128)} %bitcast.2, bf16[4096,128]{1,0:T(8,128)(2,1)} %sketch_ref.1), custom_call_target="tpu_custom_call" | custom-call | flops 4499999744 | bytes 12000000 | tf_op jit(solution)/shard_map/subspace/pallas_call | solution.py:475
  93.9 2.0 %outputs.1 = (f32[896,128]{1,0:T(8,128)}, f32[1024,128]{1,0:T(8,128)}) custom-call(f32[896,128]{1,0:T(8,128)} %get-tuple-element.4.scores_in, f32[1024,128]{1,0:T(8,128)} %get-tuple-element.5.loads_in), custom_call_target="tpu_custom_call" | custom-call | bytes 2000000 | tf_op jit(solution)/shard_map/outputs/pallas_call | solution.py:494

commit v3 on v2

--- a/solution.py
+++ b/solution.py
@@ -142,6 +142,7 @@
     for r in range(chunks):
         load(r).start()
     barrier = pltpu.get_barrier_semaphore()
+    far = sorted(range(1, Z), key=lambda k: -min(k, Z - k))
     others = [core_peer] + x_peer[1:] + y_peer[1:] + z_peer[1:]
     for other in others:
         pl.semaphore_signal(barrier, inc=1, device_id=other, device_id_type=MESH)
@@ -268,7 +269,7 @@
         for copy in gram_y:
             copy.wait_recv()
         g_z[it, z] = (g_y[it, 0] + g_y[it, 1]) + (g_y[it, 2] + g_y[it, 3])
-        gram_z = [push(g_z.at[it, z], g_z.at[it, z], z_peer[k]) for k in range(1, Z)]
+        gram_z = [push(g_z.at[it, z], g_z.at[it, z], z_peer[k]) for k in far]
 
         second_a, second_b = [], []
         for j in (1, 2, 3, 0):
@@ -297,7 +298,7 @@
             copy.wait_recv()
         zsrc[it, 0:4] = own[it, y, x, 0:4] + rx2a[it, 0] + rx2a[it, 1] + rx2a[it, 2]
         zsrc[it, 4:8] = own[it, y, x, 4:8] + rx2b[it, 0] + rx2b[it, 1] + rx2b[it, 2]
-        third = [push(zsrc.at[it, zs[k]], rxz.at[it, k - 1], z_peer[k]) for k in range(1, Z)]
+        third = [push(zsrc.at[it, zs[k]], rxz.at[it, k - 1], z_peer[k]) for k in far]
         for copy in gram_x:
             copy.wait_recv()
         g_full[it, c] = g_x[it]
@@ -312,7 +313,7 @@
         else:
             mine = fin.at[y, c, x]
         mine[z] = value
-        gather_z = [push(mine.at[z], mine.at[z], z_peer[k]) for k in range(1, Z)]
+        gather_z = [push(mine.at[z], mine.at[z], z_peer[k]) for k in far]
         gram_core.wait_recv()
         gram[...] = g_full[it].reshape(LANES, LANES)
         panels = LANES // PIVOTS

time: 96.6 us -> 95.8 us (level)
  no operation moved by 1% of the time
where the time goes in v3:
time: 95.8 us; the launch traced here: 95.6 us
  Pallas kernels  94.9 us (99%)
    pallas_call x1, Pallas kernels, on_device(): pl.pallas_call(functools.partial(kernel, samples * groups, math.sqrt(kept...  92.9 us
    pallas_call x1, Pallas kernels, on_device(): pl.pallas_call(hand_on, name='outputs', out_shape=results, in_specs=[any_...  2.04 us

profile of v3, /device:TPU:32, one launch (start us, length us, event | category | flops | bytes accessed | tf_op | source)
XLA Modules:
  0.0 95.6 jit_solution(2262990297859060175)
XLA Ops:
  0.6 92.9 %subspace.1 = (f32[896,128]{1,0:T(8,128)}, f32[1024,128]{1,0:T(8,128)}) custom-call(bf16[1024,4096]{1,0:T(8,128)(2,1)} %dose_ref.1, s32[7,128]{1,0:T(8,128)} %bitcast.3, s32[1,4096]{1,0:T(1,128)} %bitcast.2, bf16[4096,128]{1,0:T(8,128)(2,1)} %sketch_ref.1), custom_call_target="tpu_custom_call" | custom-call | flops 4499999744 | bytes 12000000 | tf_op jit(solution)/shard_map/subspace/pallas_call | solution.py:476
  93.5 2.0 %outputs.1 = (f32[896,128]{1,0:T(8,128)}, f32[1024,128]{1,0:T(8,128)}) custom-call(f32[896,128]{1,0:T(8,128)} %get-tuple-element.4.scores_in, f32[1024,128]{1,0:T(8,128)} %get-tuple-element.5.loads_in), custom_call_target="tpu_custom_call" | custom-call | bytes 2000000 | tf_op jit(solution)/shard_map/outputs/pallas_call | solution.py:495
